TPU v7x, 128 devices: a whole 4x4x4 slice. The times are simulated.
128 devices in a mesh: src: 16 (over y, z), rcv: 8 (over x, core).
Axes of the slice: x: 4, y: 4, z: 4, core: 2. Of those that a mesh axis runs over, the one named last changes fastest.
Arguments:
- traces: bfloat16 [2048, 1024], P('src', 'rcv'), may hold values from -300 to 300, as said below
- counts: int32 [16, 8], P('src', 'rcv'), may hold values from 1 to 4, as said below
- distances: int32 [4], replicated, may hold values from -8 to 7, as said below
Outputs:
- stacks: bfloat16 [16, 4, 64, 128, 2048], P('src', None, None, None, 'rcv')
Inputs may be any that keep to these rules, and one draw needn't show every extreme that they name: `counts`: each entry is at least 1 and at most 4; both ends occur. 4 distinct block distances; -8, -1 and 7 always occur. `traces`: finite values.
All inputs are finite; a program needn't handle non-finite values.
Results may differ from a plain program's by a relative error of at most 0.0057.
Values may be sent and summed in bfloat16 or wider, within the bound.
No kernel may reach another device: no remote copies, remote signals or barrier semaphores. Data moves between devices by JAX's collectives and lax.ppermute only.
A program may use at most 384 MiB of HBM per device.

v0:
```python
import functools

import jax
import jax.numpy as jnp
from jax import lax
from jax.experimental import pallas as pl
from jax.experimental.pallas import tpu as pltpu
from jax.sharding import PartitionSpec as P

LAGS = 2048
VS = 64
WIN = 32
K = 4
CB = 128
SEG = 128
NB = 16
N_RCV = 8
TIME = 1024
SHARE = 256
HALF = 512
SPAN = TIME + SHARE
GROUP = 8
COPIES = 16
FIXED = (-8, -1, 7)
OTHERS = (-7, -6, -5, -4, -3, -2, 0, 1, 2, 3, 4, 5, 6)
VMEM_BYTES = 32 * 2**20


def whiten(raw):
    values = raw.astype(jnp.float32)
    energy = jnp.sum(values * values, axis=1, keepdims=True)
    return (values * lax.rsqrt(energy / TIME + 1e-06)).astype(jnp.bfloat16)


def half_places():
    half = lax.axis_index("rcv") // 4
    return pl.multiple_of(half * HALF, HALF), pl.multiple_of((1 - half) * HALF, HALF)


def prepare_kernel(near_ref, far_ref, copies_ref, scale_ref, v_ref, own_ref):
    step = pl.program_id(0)

    @pl.when(step == 0)
    def _():
        near, far = half_places()
        own_ref[:, pl.ds(near, HALF)] = near_ref[...]
        own_ref[:, pl.ds(far, HALF)] = far_ref[...]
        counts = own_ref[CB : CB + 16, :].astype(jnp.float32)[0:1]
        norm = lax.rsqrt(jnp.sum(counts, axis=1, keepdims=True) * (WIN / SEG))
        scale_ref[...] = jnp.broadcast_to(norm, scale_ref.shape)
        lane = lax.broadcasted_iota(jnp.int32, (1, TIME), 1)
        kept = (lane % SEG).astype(jnp.float32) < counts * WIN
        sources = jnp.where(kept, whiten(own_ref[0:VS, :]).astype(jnp.float32), 0.0)
        sources = sources.astype(jnp.bfloat16)
        row = lax.broadcasted_iota(jnp.int32, (SEG, SEG), 0)
        col = lax.broadcasted_iota(jnp.int32, (SEG, SEG), 1)
        flip = jnp.where(row + col == SEG - 1, 1.0, 0.0).astype(jnp.bfloat16)
        v_ref[:, 0:TIME] = jnp.zeros((VS, TIME), jnp.float32)
        v_ref[:, 2 * TIME :] = jnp.zeros((VS, TIME), jnp.float32)
        for e in range(N_RCV):
            part = sources[:, (N_RCV - 1 - e) * SEG : (N_RCV - e) * SEG]
            v_ref[:, TIME + e * SEG : TIME + (e + 1) * SEG] = jnp.dot(
                part, flip, preferred_element_type=jnp.float32
            )

    base = pl.multiple_of(lax.axis_index("rcv") * SHARE, SHARE)
    first = pl.multiple_of(step * COPIES, COPIES)
    rows = v_ref[pl.ds(first, COPIES), pl.ds(base, SPAN)]
    spread = jnp.broadcast_to(rows[:, None, :], (COPIES, 16, SPAN))
    copies_ref[...] = pltpu.roll(spread, SPAN - 15, 2, stride=1, stride_axis=1).astype(jnp.bfloat16)


def prepare(near, far):
    return pl.pallas_call(
        prepare_kernel,
        grid=(VS // COPIES,),
        in_specs=[pl.BlockSpec((CB + 16, HALF), lambda i: (0, 0))] * 2,
        out_specs=[
            pl.BlockSpec((COPIES, 16, SPAN), lambda i: (i, 0, 0)),
            pl.BlockSpec((8, 128), lambda i: (0, 0)),
        ],
        out_shape=[
            jax.ShapeDtypeStruct((VS, 16, SPAN), jnp.bfloat16),
            jax.ShapeDtypeStruct((8, 128), jnp.float32),
        ],
        scratch_shapes=[
            pltpu.VMEM((VS, 3 * TIME), jnp.float32),
            pltpu.VMEM((CB + 16, TIME), jnp.bfloat16),
        ],
        compiler_params=pltpu.CompilerParams(vmem_limit_bytes=VMEM_BYTES),
        name="prepare",
    )(near, far)


def corr_kernel(dist_ref, copies_ref, scale_ref, *refs):
    *halves, out_ref, w_ref, q_ref = refs
    core = lax.axis_index("rcv") % 2
    block = lax.axis_index("src")
    slot_of = [jnp.int32(0)] * K
    rest = jnp.int32(0)
    fourth = jnp.int32(0)
    for k in range(K):
        d = dist_ref[k]
        fixed = jnp.bool_(False)
        for s, known in enumerate(FIXED):
            hit = d == known
            slot_of[s] = jnp.where(hit, k, slot_of[s])
            fixed = jnp.logical_or(fixed, hit)
        rest = jnp.where(fixed, rest, k)
        fourth = jnp.where(fixed, fourth, d)
    slot_of[3] = rest
    order = ((0, 1), (2, 3), (1, 0), (3, 2))
    values = (*(jnp.int32(d) for d in FIXED), fourth)
    inside = []
    for x, y in order:
        partner = block + jnp.where(core == 0, values[x], values[y])
        inside.append(jnp.logical_and(partner >= 0, partner < NB).astype(jnp.int32))
    total = sum(inside)
    ranks = []
    used, unused = jnp.int32(0), total
    for flag in inside:
        ranks.append(jnp.where(flag == 1, used, unused))
        used, unused = used + flag, unused + 1 - flag
    slots = [jnp.int32(0)] * K
    for s, (x, y) in enumerate(order):
        slot = jnp.where(core == 0, slot_of[x], slot_of[y])
        for r in range(K):
            slots[r] = jnp.where(ranks[s] == r, slot, slots[r])

    @pl.when(pl.program_id(0) == 0)
    def _():
        near, far = half_places()
        for s in range(K):
            first = halves[2 * s][...].astype(jnp.float32)
            second = halves[2 * s + 1][...].astype(jnp.float32)
            energy = jnp.sum(first * first + second * second, axis=1, keepdims=True)
            scale = lax.rsqrt(energy / TIME + 1e-06) * inside[s].astype(jnp.float32)
            rows = pl.ds(pl.multiple_of(ranks[s] * CB, CB), CB)
            w_ref[rows, pl.ds(near, HALF)] = (first * scale).astype(jnp.bfloat16)
            w_ref[rows, pl.ds(far, HALF)] = (second * scale).astype(jnp.bfloat16)

    scale = scale_ref[0:1, 0:1]

    def multiply(live):
        for ii in range(GROUP):
            copies = copies_ref[ii]
            blocks = q_ref.at[ii % 2]
            for g in range(8):
                at = 112 - 16 * g
                moved = copies[:, at : at + TIME + SEG]
                for c in range(9):
                    blocks[SEG * c + 16 * g : SEG * c + 16 * g + 16, :] = moved[
                        :, SEG * (8 - c) : SEG * (9 - c)
                    ]
            tile = jnp.concatenate([blocks[SEG : SEG + TIME], blocks[0:TIME]], axis=1)
            summed = jnp.dot(w_ref[: live * CB], tile, preferred_element_type=jnp.float32)
            stack = (summed * scale).astype(jnp.bfloat16)
            for r in range(K):
                if r < live:
                    out_ref[slots[r], ii] = stack[r * CB : (r + 1) * CB]
                else:
                    out_ref[slots[r], ii] = jnp.zeros((CB, SHARE), jnp.bfloat16)

    pl.when(total <= 2)(lambda: multiply(2))
    pl.when(total == 3)(lambda: multiply(3))
    pl.when(total == 4)(lambda: multiply(4))


def correlate(distances, copies, scale, halves):
    vmem = pl.BlockSpec((CB, HALF), lambda i: (0, 0))
    return pl.pallas_call(
        corr_kernel,
        grid=(VS // GROUP,),
        in_specs=[
            pl.BlockSpec(memory_space=pltpu.SMEM),
            pl.BlockSpec((GROUP, 16, SPAN), lambda i: (i, 0, 0)),
            pl.BlockSpec((8, 128), lambda i: (0, 0)),
            *([vmem] * len(halves)),
        ],
        out_specs=pl.BlockSpec((K, GROUP, CB, SHARE), lambda i: (0, i, 0, 0)),
        out_shape=jax.ShapeDtypeStruct((K, VS, CB, SHARE), jnp.bfloat16),
        scratch_shapes=[
            pltpu.VMEM((K * CB, TIME), jnp.bfloat16),
            pltpu.VMEM((2, TIME + SEG, SEG), jnp.bfloat16),
        ],
        compiler_params=pltpu.CompilerParams(vmem_limit_bytes=VMEM_BYTES),
        name="corr",
    )(distances, copies, scale, *halves)


def flip_rcv(x, bits):
    return lax.ppermute(x, "rcv", [(s, s ^ bits) for s in range(N_RCV)])


def own_half(x):
    place = lax.axis_index("rcv") % 4
    others = [flip_rcv(x, bits) for bits in (1, 2, 3)]
    half = jnp.zeros((x.shape[0], HALF), x.dtype)
    for bits, part in enumerate((x, *others)):
        half = lax.dynamic_update_slice(half, part, (0, (place ^ bits) * SEG))
    return half


def fetch(y, even, odd):
    pairs = [
        ((p + (odd if m % 2 else even)) % NB * N_RCV + m, p * N_RCV + m)
        for p in range(NB)
        for m in range(N_RCV)
    ]
    return lax.ppermute(y, ("src", "rcv"), pairs)


def second_fetch(own, a1, fourth):
    a2 = fetch(own, 7, fourth)
    return a2, flip_rcv(a1, 6), flip_rcv(a1, 1)


def on_device(traces, counts, distances):
    rows = jnp.concatenate(
        [traces, jnp.broadcast_to(counts.astype(jnp.bfloat16), (16, SEG))], axis=0
    )
    half = own_half(rows)
    own = half[:CB]
    a1 = fetch(own, -8, -1)
    far_half = flip_rcv(half, 6)
    fourth = jnp.sum(distances) - sum(FIXED)
    branch = jnp.where(fourth < 0, fourth + 7, fourth + 6)
    branch, a1, far_half = lax.optimization_barrier((branch, a1, far_half))
    moves = [functools.partial(second_fetch, fourth=d) for d in OTHERS]
    a2, c1, s1 = lax.switch(branch, moves, own, a1)
    c2 = flip_rcv(a2, 6)
    s2 = flip_rcv(a2, 1)
    r1 = flip_rcv(c1, 1)
    half, far_half, a2 = lax.optimization_barrier((half, far_half, a2))
    copies, scale = prepare(half, far_half)
    c2, copies = lax.optimization_barrier((c2, copies))
    r2 = flip_rcv(c2, 1)
    halves = (a1, c1, a2, c2, s1, r1, s2, r2)
    return correlate(distances, copies, scale, halves)[None]


def solution(mesh):
    in_specs = (P("src", "rcv"), P("src", "rcv"), P())
    out_specs = P("src", None, None, None, "rcv")
    return jax.shard_map(
        on_device, mesh=mesh, in_specs=in_specs, out_specs=out_specs, check_vma=False
    )
```

profile of v0, /device:TPU:17, one launch (start us, length us, event | category | flops | bytes accessed | tf_op | source)
XLA Modules:
  0.0 58.9 jit_solution(14259187565122280939)
XLA Ops:
  0.7 0.8 %fusion = (bf16[144,128]{1,0:T(8,128)(2,1)S(1)}, bf16[144,512]{1,0:T(8,128)(2,1)S(1)}) fusion(bf16[128,128]{1,0:T(8,128)(2,1)} %param.16, bf16[]{:T(256)} %bitcast, bf16[144,512]{1,0:T(8,128)(2,1)S(1)} %broadcast_in_dim.11, s32[]{:T(128)S(6)} %select_n.24), kind=kLoop, calls=%fused_computation.4 | loop fusion | bytes 106502 | tf_op jit(solution)/shard_map/concatenate | solution.py:219
  1.5 0.8 %collective-permute-start.39 = (bf16[144,128]{1,0:T(8,128)(2,1)S(1)}, bf16[144,128]{1,0:T(8,128)(2,1)S(1)}, u32[]{:S(2)}, u32[]{:S(2)}) collective-permute-start(bf16[144,128]{1,0:T(8,128)(2,1)S(1)} %get-tuple-element.109), channel_id=1, source_target_pairs={{0,1},{1,0},{2,3},{3,2},{4,5},{5,4},{6,7},{7,6},{8,9},{9,8},{10,11... | collective-permute-start | bytes 110600 | tf_op jit(solution)/shard_map/ppermute | solution.py:192
  2.2 1.2 %collective-permute-start.40 = (bf16[144,128]{1,0:T(8,128)(2,1)S(1)}, bf16[144,128]{1,0:T(8,128)(2,1)S(1)}, u32[]{:S(2)}, u32[]{:S(2)}) collective-permute-start(bf16[144,128]{1,0:T(8,128)(2,1)S(1)} %get-tuple-element.109), channel_id=1, source_target_pairs={{0,2},{1,3},{2,0},{3,1},{4,6},{5,7},{6,4},{7,5},{8,10},{9,11},{10,... | collective-permute-start | bytes 110600 | tf_op jit(solution)/shard_map/ppermute | solution.py:192
  3.4 0.5 collective-permute-start.41
  4.0 1.1 %collective-permute-done.40 = bf16[144,128]{1,0:T(8,128)(2,1)S(1)} collective-permute-done((bf16[144,128]{1,0:T(8,128)(2,1)S(1)}, bf16[144,128]{1,0:T(8,128)(2,1)S(1)}, u32[]{:S(2)}, u32[]{:S(2)}) %collective-permute-start.40) | collective-permute-done | bytes 36896 | tf_op jit(solution)/shard_map/ppermute | solution.py:192
  5.1 1.8 %collective-permute-done.41 = bf16[144,128]{1,0:T(8,128)(2,1)S(1)} collective-permute-done((bf16[144,128]{1,0:T(8,128)(2,1)S(1)}, bf16[144,128]{1,0:T(8,128)(2,1)S(1)}, u32[]{:S(2)}, u32[]{:S(2)}) %collective-permute-start.41) | collective-permute-done | bytes 36896 | tf_op jit(solution)/shard_map/ppermute | solution.py:192
  6.9 2.1 %collective-permute-start.43 = (bf16[144,512]{1,0:T(8,128)(2,1)S(1)}, bf16[144,512]{1,0:T(8,128)(2,1)S(1)}, u32[]{:S(2)}, u32[]{:S(2)}) collective-permute-start(bf16[144,512]{1,0:T(8,128)(2,1)S(1)} %constant_dynamic-update-slice_fusion.near_ref), channel_id=1, source_target_pairs={{0,6},{1,7},{2,4},{3,5},{4,2},{5,3},{6,0},{7,1},{8,14},{9,15},{10,... | collective-permute-start | bytes 442376 | tf_op jit(solution)/shard_map/ppermute | solution.py:192
  9.1 1.7 %collective-permute-start.42 = (bf16[128,512]{1,0:T(8,128)(2,1)S(1)}, bf16[128,512]{1,0:T(8,128)(2,1)S(1)}, u32[]{:S(2)}, u32[]{:S(2)}) collective-permute-start(bf16[128,512]{1,0:T(8,128)(2,1)S(1)} %slice.4), channel_id=1, source_target_pairs={{64,0},{121,1},{66,2},{123,3},{68,4},{125,5},{70,6},{127,7},{72,8}... | collective-permute-start | bytes 393224 | tf_op jit(solution)/shard_map/ppermute | solution.py:210
  10.8 1.3 %reduce_sum.9 = s32[]{:T(128)} reduce(s32[4]{0:T(128)} %dist_ref.1, s32[]{:T(128)} %constant.12.clone.1), dimensions={0}, to_apply=%region_0.1 | reduce | flops 3 | bytes 24 | tf_op jit(solution)/shard_map/reduce_sum | solution.py:226
  14.0 1.1 %collective-permute-done.42.refs_0_ = bf16[128,512]{1,0:T(8,128)(2,1)S(1)} collective-permute-done((bf16[128,512]{1,0:T(8,128)(2,1)S(1)}, bf16[128,512]{1,0:T(8,128)(2,1)S(1)}, u32[]{:S(2)}, u32[]{:S(2)}) %collective-permute-start.42) | collective-permute-done | bytes 131104 | tf_op jit(solution)/shard_map/ppermute | solution.py:210
  15.1 11.2 %conditional.1 = (bf16[128,512]{1,0:T(8,128)(2,1)}, bf16[128,512]{1,0:T(8,128)(2,1)}, bf16[128,512]{1,0:T(8,128)(2,1)}) conditional(s32[]{:T(128)} %clamp.3, (bf16[128,512]{1,0:T(8,128)(2,1)S(1)}, bf16[128,512]{1,0:T(8,128)(2,1)S(1)}) %tuple.61, (bf16[128,512]{1,0:T(8,128)(2,1)S(1)}, ...), branch_computations={%region_1.2_spmd, %region_2.3_spmd, %region_3.4_spmd, %region_4.5_... | conditional | bytes 1573008 | solution.py:230
  15.1 1.3 %collective-permute-start.18 = (bf16[128,512]{1,0:T(8,128)(2,1)S(1)}, bf16[128,512]{1,0:T(8,128)(2,1)}, u32[]{:S(2)}, u32[]{:S(2)}) collective-permute-start(bf16[128,512]{1,0:T(8,128)(2,1)S(1)} %get-tuple-element.69), channel_id=1, source_target_pairs={{56,0},{1,1},{58,2},{3,3},{60,4},{5,5},{62,6},{7,7},{64,8},{9,9},{... | collective-permute-start | bytes 393224 | tf_op jit(solution)/shard_map/cond/branch_6_fun/ppermute | solution.py:210
  16.4 3.5 %collective-permute-start.20 = (bf16[128,512]{1,0:T(8,128)(2,1)S(1)}, bf16[128,512]{1,0:T(8,128)(2,1)}, u32[]{:S(2)}, u32[]{:S(2)}) collective-permute-start(bf16[128,512]{1,0:T(8,128)(2,1)S(1)} %get-tuple-element.70), channel_id=1, source_target_pairs={{0,1},{1,0},{2,3},{3,2},{4,5},{5,4},{6,7},{7,6},{8,9},{9,8},{10,11... | collective-permute-start | bytes 393224 | tf_op jit(solution)/shard_map/cond/branch_6_fun/ppermute | solution.py:192
  20.0 0.6 %collective-permute-start.19 = (bf16[128,512]{1,0:T(8,128)(2,1)S(1)}, bf16[128,512]{1,0:T(8,128)(2,1)}, u32[]{:S(2)}, u32[]{:S(2)}) collective-permute-start(bf16[128,512]{1,0:T(8,128)(2,1)S(1)} %get-tuple-element.70), channel_id=1, source_target_pairs={{0,6},{1,7},{2,4},{3,5},{4,2},{5,3},{6,0},{7,1},{8,14},{9,15},{10,... | collective-permute-start | bytes 393224 | tf_op jit(solution)/shard_map/cond/branch_6_fun/ppermute | solution.py:192
  20.6 0.5 collective-permute-done.20
  21.1 5.3 %collective-permute-done.19 = bf16[128,512]{1,0:T(8,128)(2,1)} collective-permute-done((bf16[128,512]{1,0:T(8,128)(2,1)S(1)}, bf16[128,512]{1,0:T(8,128)(2,1)}, u32[]{:S(2)}, u32[]{:S(2)}) %collective-permute-start.19) | collective-permute-done | bytes 131104 | tf_op jit(solution)/shard_map/cond/branch_6_fun/ppermute | solution.py:192
  26.3 0.6 collective-permute-start.44
  26.9 1.2 %collective-permute-start.46 = (bf16[128,512]{1,0:T(8,128)(2,1)}, bf16[128,512]{1,0:T(8,128)(2,1)S(1)}, u32[]{:S(2)}, u32[]{:S(2)}) collective-permute-start(bf16[128,512]{1,0:T(8,128)(2,1)} %get-tuple-element.106.refs_2_), channel_id=1, source_target_pairs={{0,1},{1,0},{2,3},{3,2},{4,5},{5,4},{6,7},{7,6},{8,9},{9,8},{10,11... | collective-permute-start | bytes 393224 | tf_op jit(solution)/shard_map/ppermute | solution.py:192
  28.1 1.4 %prepare.1 = (bf16[64,16,1280]{2,1,0:T(8,128)(2,1)S(1)}, f32[8,128]{1,0:T(8,128)S(1)}) custom-call(bf16[144,512]{1,0:T(8,128)(2,1)S(1)} %constant_dynamic-update-slice_fusion.near_ref, bf16[144,512]{1,0:T(8,128)(2,1)S(1)} %collective-permute-done.43.far_ref), custom_call_target="tpu_custom_call" | custom-call | tf_op jit(solution)/shard_map/prepare/pallas_call | solution.py:74
  29.5 2.4 %collective-permute-done.44.refs_3_ = bf16[128,512]{1,0:T(8,128)(2,1)S(1)} collective-permute-done((bf16[128,512]{1,0:T(8,128)(2,1)}, bf16[128,512]{1,0:T(8,128)(2,1)S(1)}, u32[]{:S(2)}, u32[]{:S(2)}) %collective-permute-start.44) | collective-permute-done | bytes 131104 | tf_op jit(solution)/shard_map/ppermute | solution.py:192
  31.9 1.8 %collective-permute-start.47 = (bf16[128,512]{1,0:T(8,128)(2,1)S(1)}, bf16[128,512]{1,0:T(8,128)(2,1)S(1)}, u32[]{:S(2)}, u32[]{:S(2)}) collective-permute-start(bf16[128,512]{1,0:T(8,128)(2,1)S(1)} %collective-permute-done.44.refs_3_), channel_id=1, source_target_pairs={{0,1},{1,0},{2,3},{3,2},{4,5},{5,4},{6,7},{7,6},{8,9},{9,8},{10,11... | collective-permute-start | bytes 393224 | tf_op jit(solution)/shard_map/ppermute | solution.py:192
  33.7 1.0 %collective-permute-done.47.refs_7_ = bf16[128,512]{1,0:T(8,128)(2,1)S(1)} collective-permute-done((bf16[128,512]{1,0:T(8,128)(2,1)S(1)}, bf16[128,512]{1,0:T(8,128)(2,1)S(1)}, u32[]{:S(2)}, u32[]{:S(2)}) %collective-permute-start.47) | collective-permute-done | bytes 131104 | tf_op jit(solution)/shard_map/ppermute | solution.py:192
  34.7 0.7 %copy-done = s32[4]{0:T(128)S(1)} copy-done((s32[4]{0:T(128)S(1)}, s32[4]{0:T(128)}, u32[]{:S(2)}) %copy-start) | copy-done | bytes 40
  35.3 23.6 %corr.1 = bf16[4,64,128,256]{3,2,1,0:T(8,128)(2,1)} custom-call(s32[4]{0:T(128)S(1)} %copy-done, bf16[64,16,1280]{2,1,0:T(8,128)(2,1)S(1)} %get-tuple-element.103.copies_ref, f32[8,128]{1,0:T(8,128)S(1)} %get-tuple-element.104.scale_ref, bf16[128,512]{1,0:T(8,128)(2,1)S(1)} %collective-permute-done.42.refs_0_, bf16[128,512]{1,0:T(8,128)(2,1)} %get-tuple-element.105.refs_1_, ...), custom_call_target="tpu_custom_call" | custom-call | tf_op jit(solution)/shard_map/corr/pallas_call | solution.py:171
  (12 shorter events, 0.1 us)
Async XLA Ops:
  1.5 2.5 %collective-permute-start.39 = (bf16[144,128]{1,0:T(8,128)(2,1)S(1)}, bf16[144,128]{1,0:T(8,128)(2,1)S(1)}, u32[]{:S(2)}, u32[]{:S(2)}) collective-permute-start(bf16[144,128]{1,0:T(8,128)(2,1)S(1)} %get-tuple-element.109), channel_id=1, source_target_pairs={{0,1},{1,0},{2,3},{3,2},{4,5},{5,4},{6,7},{7,6},{8,9},{9,8},{10,11... | collective-permute-start | bytes 110600 | tf_op jit(solution)/shard_map/ppermute | solution.py:192
  2.2 2.8 %collective-permute-start.40 = (bf16[144,128]{1,0:T(8,128)(2,1)S(1)}, bf16[144,128]{1,0:T(8,128)(2,1)S(1)}, u32[]{:S(2)}, u32[]{:S(2)}) collective-permute-start(bf16[144,128]{1,0:T(8,128)(2,1)S(1)} %get-tuple-element.109), channel_id=1, source_target_pairs={{0,2},{1,3},{2,0},{3,1},{4,6},{5,7},{6,4},{7,5},{8,10},{9,11},{10,... | collective-permute-start | bytes 110600 | tf_op jit(solution)/shard_map/ppermute | solution.py:192
  3.4 3.4 %collective-permute-start.41 = (bf16[144,128]{1,0:T(8,128)(2,1)S(1)}, bf16[144,128]{1,0:T(8,128)(2,1)S(1)}, u32[]{:S(2)}, u32[]{:S(2)}) collective-permute-start(bf16[144,128]{1,0:T(8,128)(2,1)S(1)} %get-tuple-element.109), channel_id=1, source_target_pairs={{0,3},{1,2},{2,1},{3,0},{4,7},{5,6},{6,5},{7,4},{8,11},{9,10},{10,... | collective-permute-start | bytes 110600 | tf_op jit(solution)/shard_map/ppermute | solution.py:192
  6.9 8.2 %collective-permute-start.43 = (bf16[144,512]{1,0:T(8,128)(2,1)S(1)}, bf16[144,512]{1,0:T(8,128)(2,1)S(1)}, u32[]{:S(2)}, u32[]{:S(2)}) collective-permute-start(bf16[144,512]{1,0:T(8,128)(2,1)S(1)} %constant_dynamic-update-slice_fusion.near_ref), channel_id=1, source_target_pairs={{0,6},{1,7},{2,4},{3,5},{4,2},{5,3},{6,0},{7,1},{8,14},{9,15},{10,... | collective-permute-start | bytes 442376 | tf_op jit(solution)/shard_map/ppermute | solution.py:192
  9.1 6.1 %collective-permute-start.42 = (bf16[128,512]{1,0:T(8,128)(2,1)S(1)}, bf16[128,512]{1,0:T(8,128)(2,1)S(1)}, u32[]{:S(2)}, u32[]{:S(2)}) collective-permute-start(bf16[128,512]{1,0:T(8,128)(2,1)S(1)} %slice.4), channel_id=1, source_target_pairs={{64,0},{121,1},{66,2},{123,3},{68,4},{125,5},{70,6},{127,7},{72,8}... | collective-permute-start | bytes 393224 | tf_op jit(solution)/shard_map/ppermute | solution.py:210
  15.1 5.4 %collective-permute-start.18 = (bf16[128,512]{1,0:T(8,128)(2,1)S(1)}, bf16[128,512]{1,0:T(8,128)(2,1)}, u32[]{:S(2)}, u32[]{:S(2)}) collective-permute-start(bf16[128,512]{1,0:T(8,128)(2,1)S(1)} %get-tuple-element.69), channel_id=1, source_target_pairs={{56,0},{1,1},{58,2},{3,3},{60,4},{5,5},{62,6},{7,7},{64,8},{9,9},{... | collective-permute-start | bytes 393224 | tf_op jit(solution)/shard_map/cond/branch_6_fun/ppermute | solution.py:210
  16.4 4.7 %collective-permute-start.20 = (bf16[128,512]{1,0:T(8,128)(2,1)S(1)}, bf16[128,512]{1,0:T(8,128)(2,1)}, u32[]{:S(2)}, u32[]{:S(2)}) collective-permute-start(bf16[128,512]{1,0:T(8,128)(2,1)S(1)} %get-tuple-element.70), channel_id=1, source_target_pairs={{0,1},{1,0},{2,3},{3,2},{4,5},{5,4},{6,7},{7,6},{8,9},{9,8},{10,11... | collective-permute-start | bytes 393224 | tf_op jit(solution)/shard_map/cond/branch_6_fun/ppermute | solution.py:192
  20.0 6.4 %collective-permute-start.19 = (bf16[128,512]{1,0:T(8,128)(2,1)S(1)}, bf16[128,512]{1,0:T(8,128)(2,1)}, u32[]{:S(2)}, u32[]{:S(2)}) collective-permute-start(bf16[128,512]{1,0:T(8,128)(2,1)S(1)} %get-tuple-element.70), channel_id=1, source_target_pairs={{0,6},{1,7},{2,4},{3,5},{4,2},{5,3},{6,0},{7,1},{8,14},{9,15},{10,... | collective-permute-start | bytes 393224 | tf_op jit(solution)/shard_map/cond/branch_6_fun/ppermute | solution.py:192
  26.3 5.6 %collective-permute-start.44 = (bf16[128,512]{1,0:T(8,128)(2,1)}, bf16[128,512]{1,0:T(8,128)(2,1)S(1)}, u32[]{:S(2)}, u32[]{:S(2)}) collective-permute-start(bf16[128,512]{1,0:T(8,128)(2,1)} %get-tuple-element.106.refs_2_), channel_id=1, source_target_pairs={{0,6},{1,7},{2,4},{3,5},{4,2},{5,3},{6,0},{7,1},{8,14},{9,15},{10,... | collective-permute-start | bytes 393224 | tf_op jit(solution)/shard_map/ppermute | solution.py:192
  26.9 6.8 %collective-permute-start.46 = (bf16[128,512]{1,0:T(8,128)(2,1)}, bf16[128,512]{1,0:T(8,128)(2,1)S(1)}, u32[]{:S(2)}, u32[]{:S(2)}) collective-permute-start(bf16[128,512]{1,0:T(8,128)(2,1)} %get-tuple-element.106.refs_2_), channel_id=1, source_target_pairs={{0,1},{1,0},{2,3},{3,2},{4,5},{5,4},{6,7},{7,6},{8,9},{9,8},{10,11... | collective-permute-start | bytes 393224 | tf_op jit(solution)/shard_map/ppermute | solution.py:192
  28.1 5.6 %collective-permute-start.45 = (bf16[128,512]{1,0:T(8,128)(2,1)}, bf16[128,512]{1,0:T(8,128)(2,1)S(1)}, u32[]{:S(2)}, u32[]{:S(2)}) collective-permute-start(bf16[128,512]{1,0:T(8,128)(2,1)} %get-tuple-element.105.refs_1_), channel_id=1, source_target_pairs={{0,1},{1,0},{2,3},{3,2},{4,5},{5,4},{6,7},{7,6},{8,9},{9,8},{10,11... | collective-permute-start | bytes 393224 | tf_op jit(solution)/shard_map/ppermute | solution.py:192
  31.9 2.8 %collective-permute-start.47 = (bf16[128,512]{1,0:T(8,128)(2,1)S(1)}, bf16[128,512]{1,0:T(8,128)(2,1)S(1)}, u32[]{:S(2)}, u32[]{:S(2)}) collective-permute-start(bf16[128,512]{1,0:T(8,128)(2,1)S(1)} %collective-permute-done.44.refs_3_), channel_id=1, source_target_pairs={{0,1},{1,0},{2,3},{3,2},{4,5},{5,4},{6,7},{7,6},{8,9},{9,8},{10,11... | collective-permute-start | bytes 393224 | tf_op jit(solution)/shard_map/ppermute | solution.py:192
  34.7 0.7 %copy-start = (s32[4]{0:T(128)S(1)}, s32[4]{0:T(128)}, u32[]{:S(2)}) copy-start(s32[4]{0:T(128)} %dist_ref.1) | copy-start | bytes 52
where the time goes:
time: 58.2 us; the launch traced here: 58.9 us
  Pallas kernels  25 us (43%)
  starting transfers between devices  15.2 us (26%)
  waiting for transfers between devices  13.2 us (23%)
  between operations  2.64 us (5%)
  local copies, waits for them, and re-layouts  1.5 us (3%)
  other arithmetic  1.29 us (2%)
    pallas_call x1, Pallas kernels, correlate(): pl.pallas_call(corr_kernel, grid=(VS // GROUP,), in_specs=[pl.BlockSpec(m...  23.6 us
    ppermute x10, starting transfers between devices, flip_rcv(): return lax.ppermute(x, 'rcv', [(s, s ^ bits) for s in range(N_RCV)])  12.2 us
    ppermute x10, waiting for transfers between devices, flip_rcv(): return lax.ppermute(x, 'rcv', [(s, s ^ bits) for s in range(N_RCV)])  12.1 us
    ppermute x2, starting transfers between devices, fetch(): return lax.ppermute(y, ('src', 'rcv'), pairs)  3 us
    pallas_call x1, Pallas kernels, prepare(): pl.pallas_call(prepare_kernel, grid=(VS // COPIES,), in_specs=[pl.BlockSp...  1.41 us
    reduce_sum x1, other arithmetic, on_device(): fourth = jnp.sum(distances) - sum(FIXED)  1.29 us
  transfers between devices with their start and end apart: 12, of which 7 were waited for; matrix products, arithmetic and copies ran while one was open for 2% of the time, Pallas kernels for 2%

commit v1 on v0

v1 whole, which is shorter than its diff:
```python
import functools

import jax
import jax.numpy as jnp
from jax import lax
from jax.experimental import pallas as pl
from jax.experimental.pallas import tpu as pltpu
from jax.sharding import PartitionSpec as P

LAGS = 2048
VS = 64
WIN = 32
K = 4
CB = 128
SEG = 128
NB = 16
N_RCV = 8
TIME = 1024
SHARE = 256
HALF = 512
SPAN = TIME + SHARE
GROUP = 8
COPIES = 16
FIXED = (-8, -1, 7)
OTHERS = (-7, -6, -5, -4, -3, -2, 0, 1, 2, 3, 4, 5, 6)
VMEM_BYTES = 32 * 2**20


def whiten(raw):
    values = raw.astype(jnp.float32)
    energy = jnp.sum(values * values, axis=1, keepdims=True)
    return (values * lax.rsqrt(energy / TIME + 1e-06)).astype(jnp.bfloat16)


def at_end():
    part = lax.axis_index("rcv")
    return jnp.logical_or(part < 2, part >= N_RCV - 2)


def half_places(packed):
    half = lax.axis_index("rcv") // 4
    near = half * HALF
    if packed:
        near = jnp.where(at_end(), 0, near)
    return pl.multiple_of(near, HALF), pl.multiple_of(HALF - near, HALF)


def prepare_kernel(dist_ref, near_ref, far_ref, copies_ref, scale_ref, v_ref, own_ref):
    step = pl.program_id(0)

    @pl.when(step == 0)
    def _():
        near, far = half_places(False)
        own_ref[:, pl.ds(near, HALF)] = near_ref[...]
        own_ref[:, pl.ds(far, HALF)] = far_ref[...]
        counts = own_ref[CB : CB + 16, :].astype(jnp.float32)[0:1]
        norm = lax.rsqrt(jnp.sum(counts, axis=1, keepdims=True) * (WIN / SEG))
        line = lax.broadcasted_iota(jnp.int32, scale_ref.shape, 0)
        table = jnp.broadcast_to(norm, scale_ref.shape)
        for k in range(K):
            table = jnp.where(line == k + 1, dist_ref[k].astype(jnp.float32), table)
        scale_ref[...] = table
        lane = lax.broadcasted_iota(jnp.int32, (1, TIME), 1)
        kept = (lane % SEG).astype(jnp.float32) < counts * WIN
        sources = jnp.where(kept, whiten(own_ref[0:VS, :]).astype(jnp.float32), 0.0)
        sources = sources.astype(jnp.bfloat16)
        row = lax.broadcasted_iota(jnp.int32, (SEG, SEG), 0)
        col = lax.broadcasted_iota(jnp.int32, (SEG, SEG), 1)
        flip = jnp.where(row + col == SEG - 1, 1.0, 0.0).astype(jnp.bfloat16)
        v_ref[:, 0:TIME] = jnp.zeros((VS, TIME), jnp.float32)
        v_ref[:, 2 * TIME :] = jnp.zeros((VS, TIME), jnp.float32)
        for e in range(N_RCV):
            part = sources[:, (N_RCV - 1 - e) * SEG : (N_RCV - e) * SEG]
            v_ref[:, TIME + e * SEG : TIME + (e + 1) * SEG] = jnp.dot(
                part, flip, preferred_element_type=jnp.float32
            )

    part = lax.axis_index("rcv")
    late = jnp.where(part >= N_RCV - 2, HALF, 0)
    base = pl.multiple_of(part * SHARE - late, SHARE)
    first = pl.multiple_of(step * COPIES, COPIES)
    rows = v_ref[pl.ds(first, COPIES), pl.ds(base, SPAN)]
    spread = jnp.broadcast_to(rows[:, None, :], (COPIES, 16, SPAN))
    copies_ref[...] = pltpu.roll(spread, SPAN - 15, 2, stride=1, stride_axis=1).astype(jnp.bfloat16)


def prepare(distances, near, far):
    return pl.pallas_call(
        prepare_kernel,
        grid=(VS // COPIES,),
        in_specs=[
            pl.BlockSpec(memory_space=pltpu.SMEM),
            *[pl.BlockSpec((CB + 16, HALF), lambda i: (0, 0))] * 2,
        ],
        out_specs=[
            pl.BlockSpec((COPIES, 16, SPAN), lambda i: (i, 0, 0)),
            pl.BlockSpec((8, 128), lambda i: (0, 0)),
        ],
        out_shape=[
            jax.ShapeDtypeStruct((VS, 16, SPAN), jnp.bfloat16),
            jax.ShapeDtypeStruct((8, 128), jnp.float32),
        ],
        scratch_shapes=[
            pltpu.VMEM((VS, 3 * TIME), jnp.float32),
            pltpu.VMEM((CB + 16, TIME), jnp.bfloat16),
        ],
        compiler_params=pltpu.CompilerParams(vmem_limit_bytes=VMEM_BYTES),
        name="prepare",
    )(distances, near, far)


def corr_kernel(copies_ref, scale_ref, *refs):
    *halves, out_ref, w_ref, q_ref, plan_ref = refs

    @pl.when(pl.program_id(0) == 0)
    def _():
        core = lax.axis_index("rcv") % 2
        block = lax.axis_index("src")
        slot_of = [jnp.int32(0)] * K
        rest = jnp.int32(0)
        fourth = jnp.int32(0)
        for k in range(K):
            d = jnp.max(scale_ref[k + 1 : k + 2, :]).astype(jnp.int32)
            fixed = jnp.bool_(False)
            for s, known in enumerate(FIXED):
                hit = d == known
                slot_of[s] = jnp.where(hit, k, slot_of[s])
                fixed = jnp.logical_or(fixed, hit)
            rest = jnp.where(fixed, rest, k)
            fourth = jnp.where(fixed, fourth, d)
        slot_of[3] = rest
        order = ((0, 1), (2, 3), (1, 0), (3, 2))
        values = (*(jnp.int32(d) for d in FIXED), fourth)
        inside = []
        for x, y in order:
            partner = block + jnp.where(core == 0, values[x], values[y])
            inside.append(jnp.logical_and(partner >= 0, partner < NB).astype(jnp.int32))
        total = sum(inside)
        plan_ref[K] = total
        near, far = half_places(True)
        used, unused = jnp.int32(0), total
        for s, (x, y) in enumerate(order):
            rank = jnp.where(inside[s] == 1, used, unused)
            used, unused = used + inside[s], unused + 1 - inside[s]
            plan_ref[rank] = jnp.where(core == 0, slot_of[x], slot_of[y])
            first = halves[2 * s][...].astype(jnp.float32)
            second = halves[2 * s + 1][...].astype(jnp.float32)
            energy = jnp.sum(first * first + second * second, axis=1, keepdims=True)
            scale = lax.rsqrt(energy / TIME + 1e-06) * inside[s].astype(jnp.float32)
            rows = pl.ds(pl.multiple_of(rank * CB, CB), CB)
            w_ref[rows, pl.ds(near, HALF)] = (first * scale).astype(jnp.bfloat16)
            w_ref[rows, pl.ds(far, HALF)] = (second * scale).astype(jnp.bfloat16)

    scale = scale_ref[0:1, 0:1]
    slots = [plan_ref[r] for r in range(K)]
    total = plan_ref[K]
    end = at_end()

    def multiply(live, depth):
        count = depth // SEG + 1
        for ii in range(GROUP):
            copies = copies_ref[ii]
            blocks = q_ref.at[ii % 2]
            for g in range(8):
                for c in range(count):
                    at = 112 - 16 * g + SEG * (8 - c)
                    blocks[SEG * c + 16 * g : SEG * c + 16 * g + 16, :] = copies[:, at : at + SEG]
            tile = jnp.concatenate([blocks[SEG : SEG + depth], blocks[0:depth]], axis=1)
            summed = jnp.dot(
                w_ref[: live * CB, :depth], tile, preferred_element_type=jnp.float32
            )
            stack = (summed * scale).astype(jnp.bfloat16)
            for r in range(K):
                if r < live:
                    out_ref[slots[r], ii] = stack[r * CB : (r + 1) * CB]
                else:
                    out_ref[slots[r], ii] = jnp.zeros((CB, SHARE), jnp.bfloat16)

    for live in (2, 3, 4):
        fits = total <= 2 if live == 2 else total == live
        pl.when(jnp.logical_and(fits, end))(functools.partial(multiply, live, HALF))
        pl.when(jnp.logical_and(fits, jnp.logical_not(end)))(
            functools.partial(multiply, live, TIME)
        )


def correlate(copies, scale, halves):
    vmem = pl.BlockSpec((CB, HALF), lambda i: (0, 0))
    return pl.pallas_call(
        corr_kernel,
        grid=(VS // GROUP,),
        in_specs=[
            pl.BlockSpec((GROUP, 16, SPAN), lambda i: (i, 0, 0)),
            pl.BlockSpec((8, 128), lambda i: (0, 0)),
            *([vmem] * len(halves)),
        ],
        out_specs=pl.BlockSpec((K, GROUP, CB, SHARE), lambda i: (0, i, 0, 0)),
        out_shape=jax.ShapeDtypeStruct((K, VS, CB, SHARE), jnp.bfloat16),
        scratch_shapes=[
            pltpu.VMEM((K * CB, TIME), jnp.bfloat16),
            pltpu.VMEM((2, TIME + SEG, SEG), jnp.bfloat16),
            pltpu.SMEM((8,), jnp.int32),
        ],
        compiler_params=pltpu.CompilerParams(vmem_limit_bytes=VMEM_BYTES),
        name="corr",
    )(copies, scale, *halves)


def flip_rcv(x, bits):
    return lax.ppermute(x, "rcv", [(s, s ^ bits) for s in range(N_RCV)])


def own_half(x):
    place = lax.axis_index("rcv") % 4
    others = [flip_rcv(x, bits) for bits in (1, 2, 3)]
    half = jnp.zeros((x.shape[0], HALF), x.dtype)
    for bits, part in enumerate((x, *others)):
        half = lax.dynamic_update_slice(half, part, (0, (place ^ bits) * SEG))
    return half


def fetch(y, even, odd):
    pairs = [
        ((p + (odd if m % 2 else even)) % NB * N_RCV + m, p * N_RCV + m)
        for p in range(NB)
        for m in range(N_RCV)
    ]
    return lax.ppermute(y, ("src", "rcv"), pairs)


def second_fetch(own, a1, fourth):
    a2 = fetch(own, 7, fourth)
    return a2, flip_rcv(a1, 6), flip_rcv(a1, 1)


def on_device(traces, counts, distances):
    rows = jnp.concatenate(
        [traces, jnp.broadcast_to(counts.astype(jnp.bfloat16), (16, SEG))], axis=0
    )
    half = own_half(rows)
    own = half[:CB]
    a1 = fetch(own, -8, -1)
    fourth = jnp.sum(distances) - sum(FIXED)
    branch = jnp.where(fourth < 0, fourth + 7, fourth + 6)
    branch, ready = lax.optimization_barrier((branch, half))
    far_half = flip_rcv(ready, 6)
    moves = [functools.partial(second_fetch, fourth=d) for d in OTHERS]
    a2, c1, s1 = lax.switch(branch, moves, own, a1)
    c2 = flip_rcv(a2, 6)
    s2 = flip_rcv(a2, 1)
    r1 = flip_rcv(c1, 1)
    half, far_half, a2 = lax.optimization_barrier((half, far_half, a2))
    copies, scale = prepare(distances, half, far_half)
    c2, copies = lax.optimization_barrier((c2, copies))
    r2 = flip_rcv(c2, 1)
    halves = (a1, c1, a2, c2, s1, r1, s2, r2)
    return correlate(copies, scale, halves)[None]


def solution(mesh):
    in_specs = (P("src", "rcv"), P("src", "rcv"), P())
    out_specs = P("src", None, None, None, "rcv")
    return jax.shard_map(
        on_device, mesh=mesh, in_specs=in_specs, out_specs=out_specs, check_vma=False
    )
```

time: 58.2 us -> 53.4 us (0.918)
  the two profiles are of different devices: /device:TPU:17 before, /device:TPU:19 now
where the time goes in v1:
time: 53.4 us; the launch traced here: 53.2 us
  Pallas kernels  26.1 us (49%)
  starting transfers between devices  12.4 us (23%)
  waiting for transfers between devices  9.3 us (17%)
  between operations  2.65 us (5%)
  local copies, waits for them, and re-layouts  1.5 us (3%)
  other arithmetic  1.29 us (2%)
    pallas_call x1, Pallas kernels, correlate(): pl.pallas_call(corr_kernel, grid=(VS // GROUP,), in_specs=[pl.BlockSpec((...  24.1 us
    ppermute x10, starting transfers between devices, flip_rcv(): return lax.ppermute(x, 'rcv', [(s, s ^ bits) for s in range(N_RCV)])  8.75 us
    ppermute x10, waiting for transfers between devices, flip_rcv(): return lax.ppermute(x, 'rcv', [(s, s ^ bits) for s in range(N_RCV)])  8.36 us
    ppermute x2, starting transfers between devices, fetch(): return lax.ppermute(y, ('src', 'rcv'), pairs)  3.61 us
    pallas_call x1, Pallas kernels, prepare(): pl.pallas_call(prepare_kernel, grid=(VS // COPIES,), in_specs=[pl.BlockSp...  1.99 us
    reduce_sum x1, other arithmetic, on_device(): fourth = jnp.sum(distances) - sum(FIXED)  1.29 us
  transfers between devices with their start and end apart: 12, of which 7 were waited for; matrix products, arithmetic and copies ran while one was open for 2% of the time, Pallas kernels for 4%

profile of v1, /device:TPU:19, one launch (start us, length us, event | category | flops | bytes accessed | tf_op | source)
XLA Modules:
  0.0 53.2 jit_solution(9244441045440997959)
XLA Ops:
  0.7 0.8 %fusion = (bf16[144,128]{1,0:T(8,128)(2,1)S(1)}, bf16[144,512]{1,0:T(8,128)(2,1)S(1)}) fusion(bf16[128,128]{1,0:T(8,128)(2,1)} %param.16, bf16[]{:T(256)} %bitcast, bf16[144,512]{1,0:T(8,128)(2,1)S(1)} %broadcast_in_dim.11, s32[]{:T(128)S(6)} %select_n.24), kind=kLoop, calls=%fused_computation.4 | loop fusion | bytes 106502 | tf_op jit(solution)/shard_map/concatenate | solution.py:237
  1.5 0.8 %collective-permute-start.39 = (bf16[144,128]{1,0:T(8,128)(2,1)S(1)}, bf16[144,128]{1,0:T(8,128)(2,1)S(1)}, u32[]{:S(2)}, u32[]{:S(2)}) collective-permute-start(bf16[144,128]{1,0:T(8,128)(2,1)S(1)} %get-tuple-element.107), channel_id=1, source_target_pairs={{0,1},{1,0},{2,3},{3,2},{4,5},{5,4},{6,7},{7,6},{8,9},{9,8},{10,11... | collective-permute-start | bytes 110600 | tf_op jit(solution)/shard_map/ppermute | solution.py:210
  2.2 0.3 collective-permute-start.40
  2.5 1.5 %collective-permute-start.41 = (bf16[144,128]{1,0:T(8,128)(2,1)S(1)}, bf16[144,128]{1,0:T(8,128)(2,1)S(1)}, u32[]{:S(2)}, u32[]{:S(2)}) collective-permute-start(bf16[144,128]{1,0:T(8,128)(2,1)S(1)} %get-tuple-element.107), channel_id=1, source_target_pairs={{0,3},{1,2},{2,1},{3,0},{4,7},{5,6},{6,5},{7,4},{8,11},{9,10},{10,... | collective-permute-start | bytes 110600 | tf_op jit(solution)/shard_map/ppermute | solution.py:210
  3.9 0.0 collective-permute-done.39
  4.0 1.1 %collective-permute-done.40 = bf16[144,128]{1,0:T(8,128)(2,1)S(1)} collective-permute-done((bf16[144,128]{1,0:T(8,128)(2,1)S(1)}, bf16[144,128]{1,0:T(8,128)(2,1)S(1)}, u32[]{:S(2)}, u32[]{:S(2)}) %collective-permute-start.40) | collective-permute-done | bytes 36896 | tf_op jit(solution)/shard_map/ppermute | solution.py:210
  5.1 1.3 %collective-permute-done.41 = bf16[144,128]{1,0:T(8,128)(2,1)S(1)} collective-permute-done((bf16[144,128]{1,0:T(8,128)(2,1)S(1)}, bf16[144,128]{1,0:T(8,128)(2,1)S(1)}, u32[]{:S(2)}, u32[]{:S(2)}) %collective-permute-start.41) | collective-permute-done | bytes 36896 | tf_op jit(solution)/shard_map/ppermute | solution.py:210
  6.4 1.7 %collective-permute-start.42 = (bf16[128,512]{1,0:T(8,128)(2,1)S(1)}, bf16[128,512]{1,0:T(8,128)(2,1)S(1)}, u32[]{:S(2)}, u32[]{:S(2)}) collective-permute-start(bf16[128,512]{1,0:T(8,128)(2,1)S(1)} %slice.4), channel_id=1, source_target_pairs={{64,0},{121,1},{66,2},{123,3},{68,4},{125,5},{70,6},{127,7},{72,8}... | collective-permute-start | bytes 393224 | tf_op jit(solution)/shard_map/ppermute | solution.py:228
  8.1 1.3 %reduce_sum.9 = s32[]{:T(128)} reduce(s32[4]{0:T(128)} %dist_ref.1, s32[]{:T(128)} %constant.12.clone.1), dimensions={0}, to_apply=%region_0.1 | reduce | flops 3 | bytes 24 | tf_op jit(solution)/shard_map/reduce_sum | solution.py:243
  11.3 1.6 %collective-permute-start.44 = (bf16[144,512]{1,0:T(8,128)(2,1)S(1)}, bf16[144,512]{1,0:T(8,128)(2,1)S(1)}, u32[]{:S(2)}, u32[]{:S(2)}) collective-permute-start(bf16[144,512]{1,0:T(8,128)(2,1)S(1)} %constant_dynamic-update-slice_fusion.near_ref), channel_id=1, source_target_pairs={{0,6},{1,7},{2,4},{3,5},{4,2},{5,3},{6,0},{7,1},{8,14},{9,15},{10,... | collective-permute-start | bytes 442376 | tf_op jit(solution)/shard_map/ppermute | solution.py:210
  12.9 9.1 %conditional.1 = (bf16[128,512]{1,0:T(8,128)(2,1)}, bf16[128,512]{1,0:T(8,128)(2,1)}, bf16[128,512]{1,0:T(8,128)(2,1)}) conditional(s32[]{:T(128)} %clamp.3, (bf16[128,512]{1,0:T(8,128)(2,1)S(1)}, bf16[128,512]{1,0:T(8,128)(2,1)S(1)}) %tuple.61, (bf16[128,512]{1,0:T(8,128)(2,1)S(1)}, ...), branch_computations={%region_1.2_spmd, %region_2.3_spmd, %region_3.4_spmd, %region_4.5_... | conditional | bytes 1573008 | solution.py:248
  12.9 1.9 %collective-permute-start.33 = (bf16[128,512]{1,0:T(8,128)(2,1)S(1)}, bf16[128,512]{1,0:T(8,128)(2,1)}, u32[]{:S(2)}, u32[]{:S(2)}) collective-permute-start(bf16[128,512]{1,0:T(8,128)(2,1)S(1)} %get-tuple-element.79), channel_id=1, source_target_pairs={{56,0},{41,1},{58,2},{43,3},{60,4},{45,5},{62,6},{47,7},{64,8},{49... | collective-permute-start | bytes 393224 | tf_op jit(solution)/shard_map/cond/branch_11_fun/ppermute | solution.py:228
  14.8 2.0 %collective-permute-start.35 = (bf16[128,512]{1,0:T(8,128)(2,1)S(1)}, bf16[128,512]{1,0:T(8,128)(2,1)}, u32[]{:S(2)}, u32[]{:S(2)}) collective-permute-start(bf16[128,512]{1,0:T(8,128)(2,1)S(1)} %get-tuple-element.80), channel_id=1, source_target_pairs={{0,1},{1,0},{2,3},{3,2},{4,5},{5,4},{6,7},{7,6},{8,9},{9,8},{10,11... | collective-permute-start | bytes 393224 | tf_op jit(solution)/shard_map/cond/branch_11_fun/ppermute | solution.py:210
  16.8 0.9 %collective-permute-done.33 = bf16[128,512]{1,0:T(8,128)(2,1)} collective-permute-done((bf16[128,512]{1,0:T(8,128)(2,1)S(1)}, bf16[128,512]{1,0:T(8,128)(2,1)}, u32[]{:S(2)}, u32[]{:S(2)}) %collective-permute-start.33) | collective-permute-done | bytes 131104 | tf_op jit(solution)/shard_map/cond/branch_11_fun/ppermute | solution.py:228
  17.7 0.2 collective-permute-done.35
  17.9 4.1 %collective-permute-done.34 = bf16[128,512]{1,0:T(8,128)(2,1)} collective-permute-done((bf16[128,512]{1,0:T(8,128)(2,1)S(1)}, bf16[128,512]{1,0:T(8,128)(2,1)}, u32[]{:S(2)}, u32[]{:S(2)}) %collective-permute-start.34) | collective-permute-done | bytes 131104 | tf_op jit(solution)/shard_map/cond/branch_11_fun/ppermute | solution.py:210
  22.0 0.1 collective-permute-start.43
  22.0 1.0 %collective-permute-start.46 = (bf16[128,512]{1,0:T(8,128)(2,1)}, bf16[128,512]{1,0:T(8,128)(2,1)S(1)}, u32[]{:S(2)}, u32[]{:S(2)}) collective-permute-start(bf16[128,512]{1,0:T(8,128)(2,1)} %get-tuple-element.104.refs_2_), channel_id=1, source_target_pairs={{0,1},{1,0},{2,3},{3,2},{4,5},{5,4},{6,7},{7,6},{8,9},{9,8},{10,11... | collective-permute-start | bytes 393224 | tf_op jit(solution)/shard_map/ppermute | solution.py:210
  23.1 0.7 %copy-done = s32[4]{0:T(128)S(1)} copy-done((s32[4]{0:T(128)S(1)}, s32[4]{0:T(128)}, u32[]{:S(2)}) %copy-start) | copy-done | bytes 40
  23.7 2.0 %prepare.1 = (bf16[64,16,1280]{2,1,0:T(8,128)(2,1)S(1)}, f32[8,128]{1,0:T(8,128)S(1)}) custom-call(s32[4]{0:T(128)S(1)} %copy-done, bf16[144,512]{1,0:T(8,128)(2,1)S(1)} %constant_dynamic-update-slice_fusion.near_ref, bf16[144,512]{1,0:T(8,128)(2,1)S(1)} %collective-permute-done.44.far_ref), custom_call_target="tpu_custom_call" | custom-call | tf_op jit(solution)/shard_map/prepare/pallas_call | solution.py:88
  25.7 0.7 %collective-permute-done.43.refs_3_ = bf16[128,512]{1,0:T(8,128)(2,1)S(1)} collective-permute-done((bf16[128,512]{1,0:T(8,128)(2,1)}, bf16[128,512]{1,0:T(8,128)(2,1)S(1)}, u32[]{:S(2)}, u32[]{:S(2)}) %collective-permute-start.43) | collective-permute-done | bytes 131104 | tf_op jit(solution)/shard_map/ppermute | solution.py:210
  26.4 1.7 %collective-permute-start.47 = (bf16[128,512]{1,0:T(8,128)(2,1)S(1)}, bf16[128,512]{1,0:T(8,128)(2,1)S(1)}, u32[]{:S(2)}, u32[]{:S(2)}) collective-permute-start(bf16[128,512]{1,0:T(8,128)(2,1)S(1)} %collective-permute-done.43.refs_3_), channel_id=1, source_target_pairs={{0,1},{1,0},{2,3},{3,2},{4,5},{5,4},{6,7},{7,6},{8,9},{9,8},{10,11... | collective-permute-start | bytes 393224 | tf_op jit(solution)/shard_map/ppermute | solution.py:210
  28.1 1.0 %collective-permute-done.47.refs_7_ = bf16[128,512]{1,0:T(8,128)(2,1)S(1)} collective-permute-done((bf16[128,512]{1,0:T(8,128)(2,1)S(1)}, bf16[128,512]{1,0:T(8,128)(2,1)S(1)}, u32[]{:S(2)}, u32[]{:S(2)}) %collective-permute-start.47) | collective-permute-done | bytes 131104 | tf_op jit(solution)/shard_map/ppermute | solution.py:210
  29.1 24.1 %corr.1 = bf16[4,64,128,256]{3,2,1,0:T(8,128)(2,1)} custom-call(bf16[64,16,1280]{2,1,0:T(8,128)(2,1)S(1)} %get-tuple-element.101.copies_ref, f32[8,128]{1,0:T(8,128)S(1)} %get-tuple-element.102.scale_ref, bf16[128,512]{1,0:T(8,128)(2,1)S(1)} %collective-permute-done.42.refs_0_, bf16[128,512]{1,0:T(8,128)(2,1)} %get-tuple-element.103.refs_1_, ...), custom_call_target="tpu_custom_call" | custom-call | tf_op jit(solution)/shard_map/corr/pallas_call | solution.py:189
  (12 shorter events, 0.1 us)
Async XLA Ops:
  1.5 2.5 %collective-permute-start.39 = (bf16[144,128]{1,0:T(8,128)(2,1)S(1)}, bf16[144,128]{1,0:T(8,128)(2,1)S(1)}, u32[]{:S(2)}, u32[]{:S(2)}) collective-permute-start(bf16[144,128]{1,0:T(8,128)(2,1)S(1)} %get-tuple-element.107), channel_id=1, source_target_pairs={{0,1},{1,0},{2,3},{3,2},{4,5},{5,4},{6,7},{7,6},{8,9},{9,8},{10,11... | collective-permute-start | bytes 110600 | tf_op jit(solution)/shard_map/ppermute | solution.py:210
  2.2 2.8 %collective-permute-start.40 = (bf16[144,128]{1,0:T(8,128)(2,1)S(1)}, bf16[144,128]{1,0:T(8,128)(2,1)S(1)}, u32[]{:S(2)}, u32[]{:S(2)}) collective-permute-start(bf16[144,128]{1,0:T(8,128)(2,1)S(1)} %get-tuple-element.107), channel_id=1, source_target_pairs={{0,2},{1,3},{2,0},{3,1},{4,6},{5,7},{6,4},{7,5},{8,10},{9,11},{10,... | collective-permute-start | bytes 110600 | tf_op jit(solution)/shard_map/ppermute | solution.py:210
  2.5 3.8 %collective-permute-start.41 = (bf16[144,128]{1,0:T(8,128)(2,1)S(1)}, bf16[144,128]{1,0:T(8,128)(2,1)S(1)}, u32[]{:S(2)}, u32[]{:S(2)}) collective-permute-start(bf16[144,128]{1,0:T(8,128)(2,1)S(1)} %get-tuple-element.107), channel_id=1, source_target_pairs={{0,3},{1,2},{2,1},{3,0},{4,7},{5,6},{6,5},{7,4},{8,11},{9,10},{10,... | collective-permute-start | bytes 110600 | tf_op jit(solution)/shard_map/ppermute | solution.py:210
  6.4 6.5 %collective-permute-start.42 = (bf16[128,512]{1,0:T(8,128)(2,1)S(1)}, bf16[128,512]{1,0:T(8,128)(2,1)S(1)}, u32[]{:S(2)}, u32[]{:S(2)}) collective-permute-start(bf16[128,512]{1,0:T(8,128)(2,1)S(1)} %slice.4), channel_id=1, source_target_pairs={{64,0},{121,1},{66,2},{123,3},{68,4},{125,5},{70,6},{127,7},{72,8}... | collective-permute-start | bytes 393224 | tf_op jit(solution)/shard_map/ppermute | solution.py:228
  11.3 11.8 %collective-permute-start.44 = (bf16[144,512]{1,0:T(8,128)(2,1)S(1)}, bf16[144,512]{1,0:T(8,128)(2,1)S(1)}, u32[]{:S(2)}, u32[]{:S(2)}) collective-permute-start(bf16[144,512]{1,0:T(8,128)(2,1)S(1)} %constant_dynamic-update-slice_fusion.near_ref), channel_id=1, source_target_pairs={{0,6},{1,7},{2,4},{3,5},{4,2},{5,3},{6,0},{7,1},{8,14},{9,15},{10,... | collective-permute-start | bytes 442376 | tf_op jit(solution)/shard_map/ppermute | solution.py:210
  12.9 4.8 %collective-permute-start.33 = (bf16[128,512]{1,0:T(8,128)(2,1)S(1)}, bf16[128,512]{1,0:T(8,128)(2,1)}, u32[]{:S(2)}, u32[]{:S(2)}) collective-permute-start(bf16[128,512]{1,0:T(8,128)(2,1)S(1)} %get-tuple-element.79), channel_id=1, source_target_pairs={{56,0},{41,1},{58,2},{43,3},{60,4},{45,5},{62,6},{47,7},{64,8},{49... | collective-permute-start | bytes 393224 | tf_op jit(solution)/shard_map/cond/branch_11_fun/ppermute | solution.py:228
  14.8 3.1 %collective-permute-start.35 = (bf16[128,512]{1,0:T(8,128)(2,1)S(1)}, bf16[128,512]{1,0:T(8,128)(2,1)}, u32[]{:S(2)}, u32[]{:S(2)}) collective-permute-start(bf16[128,512]{1,0:T(8,128)(2,1)S(1)} %get-tuple-element.80), channel_id=1, source_target_pairs={{0,1},{1,0},{2,3},{3,2},{4,5},{5,4},{6,7},{7,6},{8,9},{9,8},{10,11... | collective-permute-start | bytes 393224 | tf_op jit(solution)/shard_map/cond/branch_11_fun/ppermute | solution.py:210
  16.8 5.2 %collective-permute-start.34 = (bf16[128,512]{1,0:T(8,128)(2,1)S(1)}, bf16[128,512]{1,0:T(8,128)(2,1)}, u32[]{:S(2)}, u32[]{:S(2)}) collective-permute-start(bf16[128,512]{1,0:T(8,128)(2,1)S(1)} %get-tuple-element.80), channel_id=1, source_target_pairs={{0,6},{1,7},{2,4},{3,5},{4,2},{5,3},{6,0},{7,1},{8,14},{9,15},{10,... | collective-permute-start | bytes 393224 | tf_op jit(solution)/shard_map/cond/branch_11_fun/ppermute | solution.py:210
  22.0 4.5 %collective-permute-start.43 = (bf16[128,512]{1,0:T(8,128)(2,1)}, bf16[128,512]{1,0:T(8,128)(2,1)S(1)}, u32[]{:S(2)}, u32[]{:S(2)}) collective-permute-start(bf16[128,512]{1,0:T(8,128)(2,1)} %get-tuple-element.104.refs_2_), channel_id=1, source_target_pairs={{0,6},{1,7},{2,4},{3,5},{4,2},{5,3},{6,0},{7,1},{8,14},{9,15},{10,... | collective-permute-start | bytes 393224 | tf_op jit(solution)/shard_map/ppermute | solution.py:210
  22.0 6.1 %collective-permute-start.46 = (bf16[128,512]{1,0:T(8,128)(2,1)}, bf16[128,512]{1,0:T(8,128)(2,1)S(1)}, u32[]{:S(2)}, u32[]{:S(2)}) collective-permute-start(bf16[128,512]{1,0:T(8,128)(2,1)} %get-tuple-element.104.refs_2_), channel_id=1, source_target_pairs={{0,1},{1,0},{2,3},{3,2},{4,5},{5,4},{6,7},{7,6},{8,9},{9,8},{10,11... | collective-permute-start | bytes 393224 | tf_op jit(solution)/shard_map/ppermute | solution.py:210
  23.1 5.1 %collective-permute-start.45 = (bf16[128,512]{1,0:T(8,128)(2,1)}, bf16[128,512]{1,0:T(8,128)(2,1)S(1)}, u32[]{:S(2)}, u32[]{:S(2)}) collective-permute-start(bf16[128,512]{1,0:T(8,128)(2,1)} %get-tuple-element.103.refs_1_), channel_id=1, source_target_pairs={{0,1},{1,0},{2,3},{3,2},{4,5},{5,4},{6,7},{7,6},{8,9},{9,8},{10,11... | collective-permute-start | bytes 393224 | tf_op jit(solution)/shard_map/ppermute | solution.py:210
  23.1 0.7 %copy-start = (s32[4]{0:T(128)S(1)}, s32[4]{0:T(128)}, u32[]{:S(2)}) copy-start(s32[4]{0:T(128)} %dist_ref.1) | copy-start | bytes 52
  26.4 2.7 %collective-permute-start.47 = (bf16[128,512]{1,0:T(8,128)(2,1)S(1)}, bf16[128,512]{1,0:T(8,128)(2,1)S(1)}, u32[]{:S(2)}, u32[]{:S(2)}) collective-permute-start(bf16[128,512]{1,0:T(8,128)(2,1)S(1)} %collective-permute-done.43.refs_3_), channel_id=1, source_target_pairs={{0,1},{1,0},{2,3},{3,2},{4,5},{5,4},{6,7},{7,6},{8,9},{9,8},{10,11... | collective-permute-start | bytes 393224 | tf_op jit(solution)/shard_map/ppermute | solution.py:210

commit v2 on v1

--- a/solution.py
+++ b/solution.py
@@ -19,7 +19,7 @@
 SHARE = 256
 HALF = 512
 SPAN = TIME + SHARE
-GROUP = 8
+GROUP = 16
 COPIES = 16
 FIXED = (-8, -1, 7)
 OTHERS = (-7, -6, -5, -4, -3, -2, 0, 1, 2, 3, 4, 5, 6)

time: 53.4 us -> 52.6 us (0.985)
  Pallas kernels: 26.1 us -> 25.2 us
    ppermute x10, starting transfers between devices: 8.75 us -> 10.5 us  [flip_rcv(): return lax.ppermute(x, 'rcv', [(s, s ^ bits) for s in range(N_RCV)])]
    ppermute x2, starting transfers between devices: 3.61 us -> 1.87 us  [fetch(): return lax.ppermute(y, ('src', 'rcv'), pairs)]
    ppermute x2, waiting for transfers between devices: 0.94 us -> 0.04 us  [fetch(): return lax.ppermute(y, ('src', 'rcv'), pairs)]
    ppermute x10, waiting for transfers between devices: 8.36 us -> 9.26 us  [flip_rcv(): return lax.ppermute(x, 'rcv', [(s, s ^ bits) for s in range(N_RCV)])]
    pallas_call x1, Pallas kernels: 24.1 us -> 23.2 us  [correlate(): pl.pallas_call(corr_kernel, grid=(VS // GROUP,), in_specs=[pl.BlockSpec((...]
  transfers between devices with their start and end apart: 12 -> 12, of which waited for: 7 -> 6; matrix products, arithmetic and copies ran while one was open for 2% -> 3% of each run, Pallas kernels for 4% -> 4%
where the time goes in v2:
time: 52.6 us; the launch traced here: 52.3 us
  Pallas kernels  25.2 us (48%)
  starting transfers between devices  12.4 us (24%)
  waiting for transfers between devices  9.3 us (18%)
  between operations  2.65 us (5%)
  local copies, waits for them, and re-layouts  1.5 us (3%)
  other arithmetic  1.29 us (2%)
    pallas_call x1, Pallas kernels, correlate(): pl.pallas_call(corr_kernel, grid=(VS // GROUP,), in_specs=[pl.BlockSpec((...  23.2 us
    ppermute x10, starting transfers between devices, flip_rcv(): return lax.ppermute(x, 'rcv', [(s, s ^ bits) for s in range(N_RCV)])  10.5 us
    ppermute x10, waiting for transfers between devices, flip_rcv(): return lax.ppermute(x, 'rcv', [(s, s ^ bits) for s in range(N_RCV)])  9.26 us
    pallas_call x1, Pallas kernels, prepare(): pl.pallas_call(prepare_kernel, grid=(VS // COPIES,), in_specs=[pl.BlockSp...  1.99 us
    ppermute x2, starting transfers between devices, fetch(): return lax.ppermute(y, ('src', 'rcv'), pairs)  1.87 us
    reduce_sum x1, other arithmetic, on_device(): fourth = jnp.sum(distances) - sum(FIXED)  1.29 us
  transfers between devices with their start and end apart: 12, of which 6 were waited for; matrix products, arithmetic and copies ran while one was open for 3% of the time, Pallas kernels for 4%

profile of v2, /device:TPU:19, one launch (start us, length us, event | category | flops | bytes accessed | tf_op | source)
XLA Modules:
  0.0 52.3 jit_solution(1275511557517247942)
XLA Ops:
  0.7 0.8 %fusion = (bf16[144,128]{1,0:T(8,128)(2,1)S(1)}, bf16[144,512]{1,0:T(8,128)(2,1)S(1)}) fusion(bf16[128,128]{1,0:T(8,128)(2,1)} %param.16, bf16[]{:T(256)} %bitcast, bf16[144,512]{1,0:T(8,128)(2,1)S(1)} %broadcast_in_dim.11, s32[]{:T(128)S(6)} %select_n.24), kind=kLoop, calls=%fused_computation.4 | loop fusion | bytes 106502 | tf_op jit(solution)/shard_map/concatenate | solution.py:237
  1.5 0.8 %collective-permute-start.39 = (bf16[144,128]{1,0:T(8,128)(2,1)S(1)}, bf16[144,128]{1,0:T(8,128)(2,1)S(1)}, u32[]{:S(2)}, u32[]{:S(2)}) collective-permute-start(bf16[144,128]{1,0:T(8,128)(2,1)S(1)} %get-tuple-element.107), channel_id=1, source_target_pairs={{0,1},{1,0},{2,3},{3,2},{4,5},{5,4},{6,7},{7,6},{8,9},{9,8},{10,11... | collective-permute-start | bytes 110600 | tf_op jit(solution)/shard_map/ppermute | solution.py:210
  2.2 0.3 collective-permute-start.40
  2.5 1.5 %collective-permute-start.41 = (bf16[144,128]{1,0:T(8,128)(2,1)S(1)}, bf16[144,128]{1,0:T(8,128)(2,1)S(1)}, u32[]{:S(2)}, u32[]{:S(2)}) collective-permute-start(bf16[144,128]{1,0:T(8,128)(2,1)S(1)} %get-tuple-element.107), channel_id=1, source_target_pairs={{0,3},{1,2},{2,1},{3,0},{4,7},{5,6},{6,5},{7,4},{8,11},{9,10},{10,... | collective-permute-start | bytes 110600 | tf_op jit(solution)/shard_map/ppermute | solution.py:210
  3.9 0.0 collective-permute-done.39
  4.0 1.1 %collective-permute-done.40 = bf16[144,128]{1,0:T(8,128)(2,1)S(1)} collective-permute-done((bf16[144,128]{1,0:T(8,128)(2,1)S(1)}, bf16[144,128]{1,0:T(8,128)(2,1)S(1)}, u32[]{:S(2)}, u32[]{:S(2)}) %collective-permute-start.40) | collective-permute-done | bytes 36896 | tf_op jit(solution)/shard_map/ppermute | solution.py:210
  5.1 1.3 %collective-permute-done.41 = bf16[144,128]{1,0:T(8,128)(2,1)S(1)} collective-permute-done((bf16[144,128]{1,0:T(8,128)(2,1)S(1)}, bf16[144,128]{1,0:T(8,128)(2,1)S(1)}, u32[]{:S(2)}, u32[]{:S(2)}) %collective-permute-start.41) | collective-permute-done | bytes 36896 | tf_op jit(solution)/shard_map/ppermute | solution.py:210
  6.4 1.7 %collective-permute-start.42 = (bf16[128,512]{1,0:T(8,128)(2,1)S(1)}, bf16[128,512]{1,0:T(8,128)(2,1)S(1)}, u32[]{:S(2)}, u32[]{:S(2)}) collective-permute-start(bf16[128,512]{1,0:T(8,128)(2,1)S(1)} %slice.4), channel_id=1, source_target_pairs={{64,0},{121,1},{66,2},{123,3},{68,4},{125,5},{70,6},{127,7},{72,8}... | collective-permute-start | bytes 393224 | tf_op jit(solution)/shard_map/ppermute | solution.py:228
  8.1 1.3 %reduce_sum.9 = s32[]{:T(128)} reduce(s32[4]{0:T(128)} %dist_ref.1, s32[]{:T(128)} %constant.12.clone.1), dimensions={0}, to_apply=%region_0.1 | reduce | flops 3 | bytes 24 | tf_op jit(solution)/shard_map/reduce_sum | solution.py:243
  11.3 1.6 %collective-permute-start.44 = (bf16[144,512]{1,0:T(8,128)(2,1)S(1)}, bf16[144,512]{1,0:T(8,128)(2,1)S(1)}, u32[]{:S(2)}, u32[]{:S(2)}) collective-permute-start(bf16[144,512]{1,0:T(8,128)(2,1)S(1)} %constant_dynamic-update-slice_fusion.near_ref), channel_id=1, source_target_pairs={{0,6},{1,7},{2,4},{3,5},{4,2},{5,3},{6,0},{7,1},{8,14},{9,15},{10,... | collective-permute-start | bytes 442376 | tf_op jit(solution)/shard_map/ppermute | solution.py:210
  12.9 9.1 %conditional.1 = (bf16[128,512]{1,0:T(8,128)(2,1)}, bf16[128,512]{1,0:T(8,128)(2,1)}, bf16[128,512]{1,0:T(8,128)(2,1)}) conditional(s32[]{:T(128)} %clamp.3, (bf16[128,512]{1,0:T(8,128)(2,1)S(1)}, bf16[128,512]{1,0:T(8,128)(2,1)S(1)}) %tuple.61, (bf16[128,512]{1,0:T(8,128)(2,1)S(1)}, ...), branch_computations={%region_1.2_spmd, %region_2.3_spmd, %region_3.4_spmd, %region_4.5_... | conditional | bytes 1573008 | solution.py:248
  12.9 0.2 collective-permute-start.30
  13.0 3.7 %collective-permute-start.32 = (bf16[128,512]{1,0:T(8,128)(2,1)S(1)}, bf16[128,512]{1,0:T(8,128)(2,1)}, u32[]{:S(2)}, u32[]{:S(2)}) collective-permute-start(bf16[128,512]{1,0:T(8,128)(2,1)S(1)} %get-tuple-element.78), channel_id=1, source_target_pairs={{0,1},{1,0},{2,3},{3,2},{4,5},{5,4},{6,7},{7,6},{8,9},{9,8},{10,11... | collective-permute-start | bytes 393224 | tf_op jit(solution)/shard_map/cond/branch_10_fun/ppermute | solution.py:210
  16.8 0.0 collective-permute-done.30
  16.8 1.1 %collective-permute-done.32 = bf16[128,512]{1,0:T(8,128)(2,1)} collective-permute-done((bf16[128,512]{1,0:T(8,128)(2,1)S(1)}, bf16[128,512]{1,0:T(8,128)(2,1)}, u32[]{:S(2)}, u32[]{:S(2)}) %collective-permute-start.32) | collective-permute-done | bytes 131104 | tf_op jit(solution)/shard_map/cond/branch_10_fun/ppermute | solution.py:210
  17.9 4.1 %collective-permute-done.31 = bf16[128,512]{1,0:T(8,128)(2,1)} collective-permute-done((bf16[128,512]{1,0:T(8,128)(2,1)S(1)}, bf16[128,512]{1,0:T(8,128)(2,1)}, u32[]{:S(2)}, u32[]{:S(2)}) %collective-permute-start.31) | collective-permute-done | bytes 131104 | tf_op jit(solution)/shard_map/cond/branch_10_fun/ppermute | solution.py:210
  22.0 0.1 collective-permute-start.43
  22.0 1.0 %collective-permute-start.46 = (bf16[128,512]{1,0:T(8,128)(2,1)}, bf16[128,512]{1,0:T(8,128)(2,1)S(1)}, u32[]{:S(2)}, u32[]{:S(2)}) collective-permute-start(bf16[128,512]{1,0:T(8,128)(2,1)} %get-tuple-element.104.refs_2_), channel_id=1, source_target_pairs={{0,1},{1,0},{2,3},{3,2},{4,5},{5,4},{6,7},{7,6},{8,9},{9,8},{10,11... | collective-permute-start | bytes 393224 | tf_op jit(solution)/shard_map/ppermute | solution.py:210
  23.1 0.7 %copy-done = s32[4]{0:T(128)S(1)} copy-done((s32[4]{0:T(128)S(1)}, s32[4]{0:T(128)}, u32[]{:S(2)}) %copy-start) | copy-done | bytes 40
  23.7 2.0 %prepare.1 = (bf16[64,16,1280]{2,1,0:T(8,128)(2,1)S(1)}, f32[8,128]{1,0:T(8,128)S(1)}) custom-call(s32[4]{0:T(128)S(1)} %copy-done, bf16[144,512]{1,0:T(8,128)(2,1)S(1)} %constant_dynamic-update-slice_fusion.near_ref, bf16[144,512]{1,0:T(8,128)(2,1)S(1)} %collective-permute-done.44.far_ref), custom_call_target="tpu_custom_call" | custom-call | tf_op jit(solution)/shard_map/prepare/pallas_call | solution.py:88
  25.7 0.7 %collective-permute-done.43.refs_3_ = bf16[128,512]{1,0:T(8,128)(2,1)S(1)} collective-permute-done((bf16[128,512]{1,0:T(8,128)(2,1)}, bf16[128,512]{1,0:T(8,128)(2,1)S(1)}, u32[]{:S(2)}, u32[]{:S(2)}) %collective-permute-start.43) | collective-permute-done | bytes 131104 | tf_op jit(solution)/shard_map/ppermute | solution.py:210
  26.4 1.7 %collective-permute-start.47 = (bf16[128,512]{1,0:T(8,128)(2,1)S(1)}, bf16[128,512]{1,0:T(8,128)(2,1)S(1)}, u32[]{:S(2)}, u32[]{:S(2)}) collective-permute-start(bf16[128,512]{1,0:T(8,128)(2,1)S(1)} %collective-permute-done.43.refs_3_), channel_id=1, source_target_pairs={{0,1},{1,0},{2,3},{3,2},{4,5},{5,4},{6,7},{7,6},{8,9},{9,8},{10,11... | collective-permute-start | bytes 393224 | tf_op jit(solution)/shard_map/ppermute | solution.py:210
  28.1 1.0 %collective-permute-done.47.refs_7_ = bf16[128,512]{1,0:T(8,128)(2,1)S(1)} collective-permute-done((bf16[128,512]{1,0:T(8,128)(2,1)S(1)}, bf16[128,512]{1,0:T(8,128)(2,1)S(1)}, u32[]{:S(2)}, u32[]{:S(2)}) %collective-permute-start.47) | collective-permute-done | bytes 131104 | tf_op jit(solution)/shard_map/ppermute | solution.py:210
  29.1 23.2 %corr.1 = bf16[4,64,128,256]{3,2,1,0:T(8,128)(2,1)} custom-call(bf16[64,16,1280]{2,1,0:T(8,128)(2,1)S(1)} %get-tuple-element.101.copies_ref, f32[8,128]{1,0:T(8,128)S(1)} %get-tuple-element.102.scale_ref, bf16[128,512]{1,0:T(8,128)(2,1)S(1)} %collective-permute-done.42.refs_0_, bf16[128,512]{1,0:T(8,128)(2,1)} %get-tuple-element.103.refs_1_, ...), custom_call_target="tpu_custom_call" | custom-call | tf_op jit(solution)/shard_map/corr/pallas_call | solution.py:189
  (12 shorter events, 0.1 us)
Async XLA Ops:
  1.5 2.5 %collective-permute-start.39 = (bf16[144,128]{1,0:T(8,128)(2,1)S(1)}, bf16[144,128]{1,0:T(8,128)(2,1)S(1)}, u32[]{:S(2)}, u32[]{:S(2)}) collective-permute-start(bf16[144,128]{1,0:T(8,128)(2,1)S(1)} %get-tuple-element.107), channel_id=1, source_target_pairs={{0,1},{1,0},{2,3},{3,2},{4,5},{5,4},{6,7},{7,6},{8,9},{9,8},{10,11... | collective-permute-start | bytes 110600 | tf_op jit(solution)/shard_map/ppermute | solution.py:210
  2.2 2.8 %collective-permute-start.40 = (bf16[144,128]{1,0:T(8,128)(2,1)S(1)}, bf16[144,128]{1,0:T(8,128)(2,1)S(1)}, u32[]{:S(2)}, u32[]{:S(2)}) collective-permute-start(bf16[144,128]{1,0:T(8,128)(2,1)S(1)} %get-tuple-element.107), channel_id=1, source_target_pairs={{0,2},{1,3},{2,0},{3,1},{4,6},{5,7},{6,4},{7,5},{8,10},{9,11},{10,... | collective-permute-start | bytes 110600 | tf_op jit(solution)/shard_map/ppermute | solution.py:210
  2.5 3.8 %collective-permute-start.41 = (bf16[144,128]{1,0:T(8,128)(2,1)S(1)}, bf16[144,128]{1,0:T(8,128)(2,1)S(1)}, u32[]{:S(2)}, u32[]{:S(2)}) collective-permute-start(bf16[144,128]{1,0:T(8,128)(2,1)S(1)} %get-tuple-element.107), channel_id=1, source_target_pairs={{0,3},{1,2},{2,1},{3,0},{4,7},{5,6},{6,5},{7,4},{8,11},{9,10},{10,... | collective-permute-start | bytes 110600 | tf_op jit(solution)/shard_map/ppermute | solution.py:210
  6.4 6.5 %collective-permute-start.42 = (bf16[128,512]{1,0:T(8,128)(2,1)S(1)}, bf16[128,512]{1,0:T(8,128)(2,1)S(1)}, u32[]{:S(2)}, u32[]{:S(2)}) collective-permute-start(bf16[128,512]{1,0:T(8,128)(2,1)S(1)} %slice.4), channel_id=1, source_target_pairs={{64,0},{121,1},{66,2},{123,3},{68,4},{125,5},{70,6},{127,7},{72,8}... | collective-permute-start | bytes 393224 | tf_op jit(solution)/shard_map/ppermute | solution.py:228
  11.3 11.8 %collective-permute-start.44 = (bf16[144,512]{1,0:T(8,128)(2,1)S(1)}, bf16[144,512]{1,0:T(8,128)(2,1)S(1)}, u32[]{:S(2)}, u32[]{:S(2)}) collective-permute-start(bf16[144,512]{1,0:T(8,128)(2,1)S(1)} %constant_dynamic-update-slice_fusion.near_ref), channel_id=1, source_target_pairs={{0,6},{1,7},{2,4},{3,5},{4,2},{5,3},{6,0},{7,1},{8,14},{9,15},{10,... | collective-permute-start | bytes 442376 | tf_op jit(solution)/shard_map/ppermute | solution.py:210
  12.9 3.9 %collective-permute-start.30 = (bf16[128,512]{1,0:T(8,128)(2,1)S(1)}, bf16[128,512]{1,0:T(8,128)(2,1)}, u32[]{:S(2)}, u32[]{:S(2)}) collective-permute-start(bf16[128,512]{1,0:T(8,128)(2,1)S(1)} %get-tuple-element.77), channel_id=1, source_target_pairs={{56,0},{33,1},{58,2},{35,3},{60,4},{37,5},{62,6},{39,7},{64,8},{41... | collective-permute-start | bytes 393224 | tf_op jit(solution)/shard_map/cond/branch_10_fun/ppermute | solution.py:228
  13.0 4.8 %collective-permute-start.32 = (bf16[128,512]{1,0:T(8,128)(2,1)S(1)}, bf16[128,512]{1,0:T(8,128)(2,1)}, u32[]{:S(2)}, u32[]{:S(2)}) collective-permute-start(bf16[128,512]{1,0:T(8,128)(2,1)S(1)} %get-tuple-element.78), channel_id=1, source_target_pairs={{0,1},{1,0},{2,3},{3,2},{4,5},{5,4},{6,7},{7,6},{8,9},{9,8},{10,11... | collective-permute-start | bytes 393224 | tf_op jit(solution)/shard_map/cond/branch_10_fun/ppermute | solution.py:210
  16.8 5.2 %collective-permute-start.31 = (bf16[128,512]{1,0:T(8,128)(2,1)S(1)}, bf16[128,512]{1,0:T(8,128)(2,1)}, u32[]{:S(2)}, u32[]{:S(2)}) collective-permute-start(bf16[128,512]{1,0:T(8,128)(2,1)S(1)} %get-tuple-element.78), channel_id=1, source_target_pairs={{0,6},{1,7},{2,4},{3,5},{4,2},{5,3},{6,0},{7,1},{8,14},{9,15},{10,... | collective-permute-start | bytes 393224 | tf_op jit(solution)/shard_map/cond/branch_10_fun/ppermute | solution.py:210
  22.0 4.5 %collective-permute-start.43 = (bf16[128,512]{1,0:T(8,128)(2,1)}, bf16[128,512]{1,0:T(8,128)(2,1)S(1)}, u32[]{:S(2)}, u32[]{:S(2)}) collective-permute-start(bf16[128,512]{1,0:T(8,128)(2,1)} %get-tuple-element.104.refs_2_), channel_id=1, source_target_pairs={{0,6},{1,7},{2,4},{3,5},{4,2},{5,3},{6,0},{7,1},{8,14},{9,15},{10,... | collective-permute-start | bytes 393224 | tf_op jit(solution)/shard_map/ppermute | solution.py:210
  22.0 6.1 %collective-permute-start.46 = (bf16[128,512]{1,0:T(8,128)(2,1)}, bf16[128,512]{1,0:T(8,128)(2,1)S(1)}, u32[]{:S(2)}, u32[]{:S(2)}) collective-permute-start(bf16[128,512]{1,0:T(8,128)(2,1)} %get-tuple-element.104.refs_2_), channel_id=1, source_target_pairs={{0,1},{1,0},{2,3},{3,2},{4,5},{5,4},{6,7},{7,6},{8,9},{9,8},{10,11... | collective-permute-start | bytes 393224 | tf_op jit(solution)/shard_map/ppermute | solution.py:210
  23.1 5.1 %collective-permute-start.45 = (bf16[128,512]{1,0:T(8,128)(2,1)}, bf16[128,512]{1,0:T(8,128)(2,1)S(1)}, u32[]{:S(2)}, u32[]{:S(2)}) collective-permute-start(bf16[128,512]{1,0:T(8,128)(2,1)} %get-tuple-element.103.refs_1_), channel_id=1, source_target_pairs={{0,1},{1,0},{2,3},{3,2},{4,5},{5,4},{6,7},{7,6},{8,9},{9,8},{10,11... | collective-permute-start | bytes 393224 | tf_op jit(solution)/shard_map/ppermute | solution.py:210
  23.1 0.7 %copy-start = (s32[4]{0:T(128)S(1)}, s32[4]{0:T(128)}, u32[]{:S(2)}) copy-start(s32[4]{0:T(128)} %dist_ref.1) | copy-start | bytes 52
  26.4 2.7 %collective-permute-start.47 = (bf16[128,512]{1,0:T(8,128)(2,1)S(1)}, bf16[128,512]{1,0:T(8,128)(2,1)S(1)}, u32[]{:S(2)}, u32[]{:S(2)}) collective-permute-start(bf16[128,512]{1,0:T(8,128)(2,1)S(1)} %collective-permute-done.43.refs_3_), channel_id=1, source_target_pairs={{0,1},{1,0},{2,3},{3,2},{4,5},{5,4},{6,7},{7,6},{8,9},{9,8},{10,11... | collective-permute-start | bytes 393224 | tf_op jit(solution)/shard_map/ppermute | solution.py:210
